TPU v7x, 256 devices: a whole 4x4x8 slice. The times are simulated.
256 devices in a mesh: blk: 32 (over y, z), col: 8 (over x, core).
Axes of the slice: x: 4, y: 4, z: 8, core: 2. Of those that a mesh axis runs over, the one named last changes fastest.
Arguments:
- right_side: float32 [64, 2048, 128], P('blk'), may hold values from -6 to 6
- below_blocks: float32 [64, 3, 128, 2048], P('blk', None, None, 'col'), may hold values from -0.09375 to 0.09375
- diag_cols: float32 [64, 2048, 128], P('blk', 'col'), as said below
- tile_home: int32 [48], replicated, may hold values from 0 to 63, as said below
- block_rows: int32 [3, 32], replicated, may hold values from 0 to 47, as said below
- block_counts: int32 [3], replicated, may hold values from 0 to 32, as said below
Outputs:
- solution: float32 [64, 2048, 128], P('blk', 'col')
Inputs may be any that keep to these rules, and one draw needn't show every extreme that they name: `tile_home`: distinct slots. For each supernode s, entries 0 to block_counts[s] - 1 of block_rows[s] are distinct tiles of supernodes after s; the remaining entries are arbitrary tiles. block_counts[0] is 32, block_counts[2] is 0, and block_counts[s] is at most (2 - s) * 16. For a tile t, diag_cols[tile_home[t]] is zero at rows i and columns j with i < (t % 16) * 128 + j.
All inputs are finite; a program needn't handle non-finite values.
Results may differ from a plain program's by a relative error of at most 0.0001.
Values sent between devices are 32-bit elements; how exact they have to be, the bound alone decides.
A program may use at most 64 MiB of HBM per device.

v0:
```python
import jax
import jax.numpy as jnp
from jax import lax
from jax.sharding import PartitionSpec as P

TILE = 128
SUPERS = 3
SAMPLES = 2048
TILES_SUP = 16
TILES = 48
MAX_BELOW = 32


def slot_layout(tile_home, block_rows, block_counts, slot_dev, blk_index):
    global_slot = blk_index * slot_dev + jnp.arange(slot_dev, dtype=jnp.int32)
    matched = tile_home[None, :] == global_slot[:, None]
    has_tile = jnp.any(matched, axis=1)
    tile_ids = jnp.arange(TILES, dtype=jnp.int32)
    tile_of = jnp.sum(jnp.where(matched, tile_ids[None, :], 0), axis=1)
    live_rows = jnp.arange(MAX_BELOW, dtype=jnp.int32)[None, :] < block_counts[:, None]
    matches = (block_rows[None, :, :] == tile_of[:, None, None]) & live_rows[None, :, :]
    present = (jnp.any(matches, axis=2) & has_tile[:, None]).astype(jnp.float32)
    return (has_tile, tile_of // TILES_SUP, tile_of % TILES_SUP, present)


def body(right_side, below_blocks, diag_cols, tile_home, block_rows, block_counts):
    precise = lax.Precision.HIGHEST
    slot_dev = below_blocks.shape[0]
    wide_cols = below_blocks.shape[3]
    tiles_col = wide_cols // TILE
    samp_col = SAMPLES // lax.axis_size("col")
    col_index = lax.axis_index("col")
    has_tile, super_of, within, present = slot_layout(
        tile_home, block_rows, block_counts, slot_dev, lax.axis_index("blk")
    )
    solution = jnp.zeros((slot_dev, samp_col, TILE), jnp.float32)
    gathered = jnp.zeros((slot_dev, SAMPLES, TILE), jnp.float32)
    local_cols = jnp.arange(tiles_col, dtype=jnp.int32)
    for level_now in range(SUPERS - 1, -1, -1):
        in_level = (has_tile & (super_of == level_now)).astype(jnp.float32)
        owned = in_level * (within // tiles_col == col_index).astype(jnp.float32)
        placing = owned[:, None] * (within[:, None] % tiles_col == local_cols[None, :]).astype(
            jnp.float32
        )
        partial_value = jnp.einsum("ju,jsb->sub", placing, right_side, precision=precise).reshape(
            SAMPLES, wide_cols
        )
        if level_now < SUPERS - 1:
            weighted = gathered * present[:, level_now][:, None, None]
            partial_value = partial_value - jnp.einsum(
                "jsb,jbw->sw", weighted, below_blocks[:, level_now], precision=precise
            )
        residual = lax.psum(partial_value, "blk")
        products = (
            jnp.einsum("sw,jwb->jsb", residual, diag_cols, precision=precise)
            * in_level[:, None, None]
        )
        solved = lax.psum_scatter(products, "col", scatter_dimension=1, tiled=True)
        solution = solution + solved
        if level_now > 0:
            gathered = gathered + lax.all_gather(solved, "col", axis=1, tiled=True)
    return solution


def solution(mesh):
    return jax.shard_map(
        body,
        mesh=mesh,
        in_specs=(
            P("blk", None, None),
            P("blk", None, None, "col"),
            P("blk", "col", None),
            P(),
            P(),
            P(),
        ),
        out_specs=P("blk", "col", None),
        check_vma=False,
    )
```

profile of v0, /device:TPU:1, one launch (start us, length us, event | category | flops | bytes accessed | tf_op | source)
XLA Modules:
  0.0 679.6 jit_solution(4005540909560969116)
XLA Ops:
  6.5 1.0 compare_reduce_fusion
  7.5 0.8 fusion.23
  8.4 14.0 %fusion.15 = f32[2,2048,128]{2,0,1:T(2,128)S(1)} fusion(f32[2,2048,128]{2,1,0:T(8,128)S(1)} %copy-done, f32[2]{0:T(128)S(1)} %get-tuple-element.12, s32[2]{0:T(128)S(1)} %and_select_fusion.2), kind=kOutput, calls=%fused_computation.21 | convolution fusion | flops 12582920 | bytes 4194320 | tf_op jit(solution)/shard_map/ju,jsb->sub/dot_general | solution.py:45
  22.4 1.4 copy.32
  23.9 153.7 %all-reduce.4.cloned.1.call-done = f32[2048,256]{1,0:T(8,128)} async-done(((f32[2048,256]{1,0:T(8,128)}), f32[2048,256]{1,0:T(8,128)}) %all-reduce.4.cloned.1.call-update) | async-done | bytes 2097168 | tf_op jit(solution)/shard_map/psum | solution.py:53
  177.6 4.7 fusion.2
  182.3 34.9 %reduce-scatter.4.cloned.1.call-done = f32[2,256,128]{2,1,0:T(8,128)} async-done(((f32[2,2048,128]{2,1,0:T(8,128)}), f32[2,256,128]{2,1,0:T(8,128)}) %reduce-scatter.4.cloned.1.call-update) | async-done | bytes 262160 | tf_op jit(solution)/shard_map/reduce_scatter | solution.py:58
  217.3 0.2 all-reduce.6.cloned.1.call-start
  217.6 0.2 and_reduce_fusion
  217.9 0.2 slice_reduce_fusion
  218.1 14.9 %fusion.13 = f32[2,2048,128]{2,0,1:T(2,128)} fusion(f32[2,2048,128]{2,1,0:T(8,128)S(1)} %copy-done, f32[2]{0:T(128)S(1)} %get-tuple-element.7, s32[2]{0:T(128)S(1)} %and_select_fusion.2), kind=kOutput, calls=%fused_computation.19 | convolution fusion | flops 12582920 | bytes 4194320 | tf_op jit(solution)/shard_map/ju,jsb->sub/dot_general | solution.py:45
  233.0 15.9 %all-gather.3.cloned.1.call-done = f32[2,2048,128]{2,1,0:T(8,128)} async-done(((f32[2,256,128]{2,1,0:T(8,128)}), f32[2,2048,128]{2,1,0:T(8,128)}) %all-gather.3.cloned.1.call-update) | async-done | bytes 2097168 | tf_op jit(solution)/shard_map/all_gather | solution.py:61
  248.9 5.4 fusion.3
  254.4 149.9 %all-reduce.6.cloned.1.call-done = f32[2048,256]{1,0:T(8,128)} async-done(((f32[2048,256]{1,0:T(8,128)}), f32[2048,256]{1,0:T(8,128)}) %all-reduce.6.cloned.1.call-update) | async-done | bytes 2097168 | tf_op jit(solution)/shard_map/psum | solution.py:53
  404.3 4.7 fusion.1
  409.1 35.0 %reduce-scatter.6.cloned.1.call-done = f32[2,256,128]{2,1,0:T(8,128)} async-done(((f32[2,2048,128]{2,1,0:T(8,128)}), f32[2,256,128]{2,1,0:T(8,128)}) %reduce-scatter.6.cloned.1.call-update) | async-done | bytes 262160 | tf_op jit(solution)/shard_map/reduce_scatter | solution.py:58
  444.0 0.3 all-reduce.8.cloned.1.call-start
  444.3 14.9 %fusion.11 = f32[2,2048,128]{2,0,1:T(2,128)} fusion(f32[2,2048,128]{2,1,0:T(8,128)S(1)} %copy-done, f32[2]{0:T(128)S(1)} %get-tuple-element.16, s32[2]{0:T(128)S(1)} %and_select_fusion.2), kind=kOutput, calls=%fused_computation.17 | convolution fusion | flops 12582920 | bytes 4194320 | tf_op jit(solution)/shard_map/ju,jsb->sub/dot_general | solution.py:45
  459.2 16.2 %all-gather.5.cloned.1.call-done = f32[2,2048,128]{2,1,0:T(8,128)} async-done(((f32[2,256,128]{2,1,0:T(8,128)}), f32[2,2048,128]{2,1,0:T(8,128)}) %all-gather.5.cloned.1.call-update) | async-done | bytes 2097168 | tf_op jit(solution)/shard_map/all_gather | solution.py:61
  475.4 6.0 fusion.4
  481.5 149.9 %all-reduce.8.cloned.1.call-done = f32[2048,256]{1,0:T(8,128)} async-done(((f32[2048,256]{1,0:T(8,128)}), f32[2048,256]{1,0:T(8,128)}) %all-reduce.8.cloned.1.call-update) | async-done | bytes 2097168 | tf_op jit(solution)/shard_map/psum | solution.py:53
  631.3 4.7 fusion
  636.0 35.0 %reduce-scatter.8.cloned.1.call-done = f32[2,256,128]{2,1,0:T(8,128)} async-done(((f32[2,2048,128]{2,1,0:T(8,128)}), f32[2,256,128]{2,1,0:T(8,128)}) %reduce-scatter.8.cloned.1.call-update) | async-done | bytes 262160 | tf_op jit(solution)/shard_map/reduce_scatter | solution.py:58
  671.0 1.7 add_add_fusion
  (34 shorter events, 0.6 us)
Async XLA Ops:
  6.5 1.9 copy-start
  6.5 171.0 %all-reduce.4.cloned.1.call-start = ((), (), s32[]{:S(2)}) async-start(), calls=%async_computation.3 | async-start | bytes 4194304 | tf_op jit(solution)/shard_map/psum | solution.py:53
  23.8 153.7 %copy-start.1 = (f32[2,256,128]{2,1,0:T(8,128)S(1)}, f32[2,256,128]{2,1,0:T(8,128)}, u32[]{:S(2)}) copy-start(f32[2,256,128]{2,1,0:T(8,128)} %param.8) | copy-start | bytes 786436
  23.9 193.4 %reduce-scatter.4.cloned.1.call-start = ((), (), s32[]{:S(2)}) async-start(), calls=%async_computation.4 | async-start | bytes 2359296 | tf_op jit(solution)/shard_map/reduce_scatter | solution.py:58
  182.3 35.3 %copy-start.6 = (s32[3]{0:T(128)S(1)}, s32[3]{0:T(128)}, u32[]{:S(2)}) copy-start(s32[3]{0:T(128)} %param.11) | copy-start | bytes 40
  182.3 35.4 %copy-start.5 = (s32[3,32]{1,0:T(4,128)S(1)}, s32[3,32]{1,0:T(4,128)}, u32[]{:S(2)}) copy-start(s32[3,32]{1,0:T(4,128)} %param.10) | copy-start | bytes 1156
  182.3 66.6 %all-gather.3.cloned.1.call-start = ((), (), s32[]{:S(2)}) async-start(), calls=%async_computation.5 | async-start | bytes 2359296 | tf_op jit(solution)/shard_map/all_gather | solution.py:61
  217.3 186.9 %all-reduce.6.cloned.1.call-start = ((), (), s32[]{:S(2)}) async-start(), calls=%async_computation.6 | async-start | bytes 4194304 | tf_op jit(solution)/shard_map/psum | solution.py:53
  218.1 30.8 %copy-start.4 = (f32[2,3,128,256]{3,2,1,0:T(8,128)S(1)}, f32[2,3,128,256]{3,2,1,0:T(8,128)}, u32[]{:S(2)}) copy-start(f32[2,3,128,256]{3,2,1,0:T(8,128)} %param.7) | copy-start | bytes 2359300
  254.3 189.7 %reduce-scatter.6.cloned.1.call-start = ((), (), s32[]{:S(2)}) async-start(), calls=%async_computation.7 | async-start | bytes 2359296 | tf_op jit(solution)/shard_map/reduce_scatter | solution.py:58
  409.0 66.4 %all-gather.5.cloned.1.call-start = ((), (), s32[]{:S(2)}) async-start(), calls=%async_computation.8 | async-start | bytes 2359296 | tf_op jit(solution)/shard_map/all_gather | solution.py:61
  444.0 187.3 %all-reduce.8.cloned.1.call-start = ((), (), s32[]{:S(2)}) async-start(), calls=%async_computation.9 | async-start | bytes 4194304 | tf_op jit(solution)/shard_map/psum | solution.py:53
  481.4 189.6 %reduce-scatter.8.cloned.1.call-start = ((), (), s32[]{:S(2)}) async-start(), calls=%async_computation.10 | async-start | bytes 2359296 | tf_op jit(solution)/shard_map/reduce_scatter | solution.py:58
  636.0 35.0 %copy-start.2 = (f32[2,256,128]{2,1,0:T(8,128)S(1)}, f32[2,256,128]{2,1,0:T(8,128)}, u32[]{:S(2)}) copy-start(f32[2,256,128]{2,1,0:T(8,128)} %reduce-scatter.4.cloned.1.call-done) | copy-start | bytes 786436
  636.0 35.0 %copy-start.3 = (f32[2,256,128]{2,1,0:T(8,128)S(1)}, f32[2,256,128]{2,1,0:T(8,128)}, u32[]{:S(2)}) copy-start(f32[2,256,128]{2,1,0:T(8,128)} %reduce-scatter.6.cloned.1.call-done) | copy-start | bytes 786436
Sparse Core Ops, SparseCore 0:
  24.0 153.5 all-reduce.3
  182.4 34.8 reduce-scatter.3
  219.3 29.5 all-gather.2
  254.5 149.7 all-reduce.5
  409.1 34.8 reduce-scatter.5
  445.7 29.6 all-gather.4
  481.5 149.7 all-reduce.7
  636.2 34.8 reduce-scatter.7
where the time goes:
time: 681 us; the launch traced here: 680 us
  waiting for transfers between devices  590 us (87%)
  matrix products  69.3 us (10%)
  between operations  13.6 us (2%)
    psum x3, waiting for transfers between devices, body(): residual = lax.psum(partial_value, 'blk')  453 us
    reduce_scatter x3, waiting for transfers between devices, body(): solved = lax.psum_scatter(products, 'col', scatter_dimension=1, tiled=True)  105 us
    dot_general x3, matrix products, body(): jnp.einsum('ju,jsb->sub', placing, right_side, precision=precise)  43.8 us
    all_gather x2, waiting for transfers between devices, body(): gathered = gathered + lax.all_gather(solved, 'col', axis=1, tiled=True)  32 us
    dot_general x3, matrix products, body(): jnp.einsum('sw,jwb->jsb', residual, diag_cols, precision=precise)  14.1 us
  transfers between devices with their start and end apart: 8, of which 8 were waited for; matrix products, arithmetic and copies ran while one was open for 4% of the time, Pallas kernels for 0%

commit v1 on v0

v1 whole, which is shorter than its diff:
```python
import functools

import jax
import jax.numpy as jnp
from jax import lax
from jax.experimental import pallas as pl
from jax.experimental.pallas import tpu as pltpu
from jax.sharding import PartitionSpec as P

TILE = 128
SUPERS = 3
SAMPLES = 2048
TILES_SUP = 16
TILES = 48
MAX_BELOW = 32
NX, NY, NZ = 4, 4, 8
ROWS = 128
HALF = 64
MESH = pl.DeviceIdType.MESH
F32 = jnp.float32
BF16 = jnp.bfloat16


def masks(tile_home, block_rows, block_counts):
    z = lax.axis_index("blk") % NZ
    core = lax.axis_index("col") % 2
    order = jnp.arange(8, dtype=jnp.int32)
    slots = ((order // 2) * NZ + z) * 2 + order % 2
    matched = tile_home[None, :] == slots[:, None]
    tile_of = jnp.max(jnp.where(matched, jnp.arange(TILES, dtype=jnp.int32)[None, :], -1), axis=1)
    levels = jnp.arange(SUPERS, dtype=jnp.int32)
    in_level = (tile_of[None, :] // TILES_SUP == levels[:, None]) & (tile_of >= 0)[None, :]
    cols = 4 * (order // 2) + 2 * core + order % 2
    placing = in_level[:, None, :] & (tile_of % TILES_SUP == cols[:, None])[None, :, :]
    live = jnp.arange(MAX_BELOW, dtype=jnp.int32)[None, :] < block_counts[:, None]
    hits = (block_rows[:, :, None] == tile_of[None, None, :]) & live[:, :, None]
    present = jnp.any(hits, axis=1)
    both = jnp.stack([in_level, present], axis=1)
    return jnp.concatenate([placing, both], axis=1).astype(F32).reshape(SUPERS * 10 * 8)


def split(v):
    hi = v.astype(BF16)
    return hi, (v - hi.astype(F32)).astype(BF16)


def kernel(
    mask, rhs, below, diag, out,
    b8, df0, df1, lf0, lf1, dhi, dlo, lhi, llo, xhi, xlo,
    part, rbuf, chunk, res, spart, exch, exch0, sol, outs, outr,
    send, recv, local,
):
    blk, col = lax.axis_index("blk"), lax.axis_index("col")
    y, z = blk // NZ, blk % NZ
    x, k = col // 2, col % 2
    count = [0, 0]

    def at(dy=0, dz=0, dx=0, dk=0):
        return (((y + dy) % NY) * NZ + (z + dz) % NZ, ((x + dx) % NX) * 2 + (k + dk) % 2)

    def push(src, dst, **where):
        i = count[0]
        count[0] += 1
        c = pltpu.make_async_remote_copy(
            src_ref=src, dst_ref=dst, send_sem=send.at[i], recv_sem=recv.at[i],
            device_id=at(**where), device_id_type=MESH,
        )
        c.start()
        sent.append(c)
        return c

    def keep(src, dst):
        i = count[1]
        count[1] += 1
        c = pltpu.make_async_copy(src, dst, local.at[i])
        c.start()
        return c

    sent = []
    own = [keep(diag.at[0], df0.at[y, x]), keep(diag.at[1], df1.at[x, y])]
    own_b = []
    for h in range(2):
        start = pl.multiple_of((2 * x + h) * 256 + y * HALF, HALF)
        own_b.append(keep(rhs.at[:, pl.ds(start, HALF), :], b8.at[y, :, pl.ds(h * HALF, HALF), :]))
    own_l = []
    for s in (1, 0):
        own_l.append(
            [keep(below.at[0, s], lf0.at[s, y, x]), keep(below.at[1, s], lf1.at[s, x, y])]
        )

    peers = [dict(dy=d) for d in range(1, NY)] + [dict(dx=d) for d in range(1, NX)]
    peers += [dict(dz=d) for d in range(1, NZ)] + [dict(dk=1)]
    barrier = pltpu.get_barrier_semaphore()
    for p in peers:
        pl.semaphore_signal(barrier, inc=1, device_id=at(**p), device_id_type=MESH)
    pl.semaphore_wait(barrier, len(peers))

    bcopies = []
    for d in (1, 3, 2):
        for h in range(2):
            start = pl.multiple_of((2 * x + h) * 256 + ((y + d) % NY) * HALF, HALF)
            bcopies.append(
                push(
                    rhs.at[:, pl.ds(start, HALF), :],
                    b8.at[y, :, pl.ds(h * HALF, HALF), :],
                    dy=d,
                )
            )

    def first(src0, dst0, src1, dst1):
        cs = []
        for d in (1, 3, 2):
            cs.append(push(src0, dst0, dx=d))
            cs.append(push(src1, dst1, dy=d))
        return cs

    def second(src0, src1):
        cs = []
        for d in (1, 3, 2):
            cs.append(push(src0, src0, dy=d))
            cs.append(push(src1, src1, dx=d))
        return cs

    def arrive(cs):
        for c in cs:
            c.wait_recv()

    d_first = first(diag.at[0], df0.at[y, x], diag.at[1], df1.at[x, y])

    for c in own_b:
        c.wait()
    arrive(bcopies)

    def place(s):
        def tile(t, carry):
            acc = jnp.zeros((ROWS, TILE), F32)
            for i in range(8):
                acc = acc + b8[i // 2, i % 2] * mask[(s * 10 + t) * 8 + i]
            part[s, t] = acc
            return carry

        lax.fori_loop(0, 8, tile, 0)

    def scatter(s):
        cs = []
        for d in (4, 3, 5, 2, 6, 1, 7):
            cs.append(push(part.at[s, (z + d) % NZ], rbuf.at[s, d - 1], dz=d))
        return cs

    def reduce(s):
        total = part[s, z]
        for d in range(1, NZ):
            total = total + rbuf[s, d - 1]
        chunk[s] = total
        res[s, z] = total

    def gather(s):
        cs = []
        for d in (4, 3, 5, 2, 6, 1, 7):
            cs.append(push(chunk.at[s], res.at[s, z], dz=d))
        return cs

    place(2)
    rs = scatter(2)

    for c in own:
        c.wait()
    arrive(d_first)
    d_second = second(df0.at[y], df1.at[x])
    l1_first = first(below.at[0, 1], lf0.at[1, y, x], below.at[1, 1], lf1.at[1, x, y])
    place(1)
    place(0)
    arrive(rs)
    reduce(2)
    ag = gather(2)
    arrive(d_second)
    for c in own_l[0]:
        c.wait()
    arrive(l1_first)
    l1_second = second(lf0.at[1, y], lf1.at[1, x])
    l0_first = first(below.at[0, 0], lf0.at[0, y, x], below.at[1, 0], lf1.at[0, x, y])

    def convert_d(i, carry):
        a, b = i // 4, i % 4
        rows = pl.ds(pl.multiple_of(b * 256, 256), 256)
        for j, v in ((0, df0[a, b]), (1, df1[b, a])):
            hi, lo = split(v)
            dhi[a, rows, j * TILE:(j + 1) * TILE] = hi
            dlo[a, rows, j * TILE:(j + 1) * TILE] = lo
        return carry

    def convert_l(s):
        def step(i, carry):
            a, b = i // 4, i % 4
            for j, v in ((0, lf0[s, a, b]), (1, lf1[s, b, a])):
                hi, lo = split(v)
                rows = pl.ds(pl.multiple_of(a * 256 + j * TILE, TILE), TILE)
                lhi[b, rows, :] = hi
                llo[b, rows, :] = lo
            return carry

        lax.fori_loop(0, 16, step, 0)

    def product(whi, wlo, n):
        a, b = xhi[...], xlo[...]
        w = whi[n]
        acc = jnp.dot(a, w, preferred_element_type=F32)
        acc = acc + jnp.dot(b, w, preferred_element_type=F32)
        return acc + jnp.dot(a, wlo[n], preferred_element_type=F32)

    def diag_step(s):
        for t in range(8):
            hi, lo = split(res[s, t])
            xhi[:, t * TILE:(t + 1) * TILE] = hi
            xlo[:, t * TILE:(t + 1) * TILE] = lo

        def step(n, carry):
            spart[s, n] = product(dhi, dlo, n)
            return carry

        lax.fori_loop(0, 4, step, 0)

    def lanes(s, row, n):
        lane = lax.broadcasted_iota(jnp.int32, (1, 256), 1)
        base = (s * 10 + row) * 8 + 2 * n
        return jnp.where(lane < TILE, mask[base], mask[base + 1])

    def absorb(s, target):
        def step(n, carry):
            v = jnp.where(lanes(s, 8, n) > 0.5, spart[s, n] + exch[s, n], 0.0)
            if s < SUPERS - 1:
                v = v + sol[n]
            sol[n] = v
            hi, lo = split(v * lanes(target, 9, n))
            where = pl.ds(pl.multiple_of(n * 256, 256), 256)
            xhi[:, where] = hi
            xlo[:, where] = lo
            return carry

        lax.fori_loop(0, 4, step, 0)

    def below_step(s):
        def step(n, carry):
            acc = product(lhi, llo, n)
            part[s, 2 * n] = part[s, 2 * n] - acc[:, :TILE]
            part[s, 2 * n + 1] = part[s, 2 * n + 1] - acc[:, TILE:]
            return carry

        lax.fori_loop(0, 4, step, 0)

    lax.fori_loop(0, 16, convert_d, 0)
    arrive(ag)
    diag_step(2)
    ex = push(spart.at[2], exch.at[2], dk=1)
    for c in own_l[1]:
        c.wait()
    arrive(l0_first)
    arrive(l1_second)
    l0_second = second(lf0.at[0, y], lf1.at[0, x])
    convert_l(1)
    ex.wait_recv()
    absorb(2, 1)
    below_step(1)
    rs = scatter(1)
    arrive(rs)
    reduce(1)
    ag = gather(1)
    arrive(l0_second)
    convert_l(0)
    arrive(ag)
    diag_step(1)
    ex = push(spart.at[1], exch.at[1], dk=1)
    ex.wait_recv()
    absorb(1, 0)
    below_step(0)
    rs = scatter(0)
    arrive(rs)
    reduce(0)
    ag = gather(0)
    arrive(ag)
    diag_step(0)
    other = pl.ds(pl.multiple_of((1 - k) * HALF, HALF), HALF)
    mine = pl.ds(pl.multiple_of(k * HALF, HALF), HALF)
    ex = push(spart.at[0, :, other, :], exch0, dk=1)
    ex.wait_recv()
    for n in range(4):
        v = spart[0, n, mine, :] + exch0[n]
        v = sol[n, mine, :] + jnp.where(lanes(0, 8, n) > 0.5, v, 0.0)
        outs[n, 0] = v[:, :TILE]
        outs[n, 1] = v[:, TILE:]
    oc = [push(outs.at[(y + d) % NY], outr.at[y], dy=d) for d in (1, 3, 2)]
    outr[y] = outs[y]
    arrive(oc)
    for n in range(4):
        for j in range(2):
            out[j, n * HALF:(n + 1) * HALF, :] = outr[n, j]
    for c in sent:
        c.wait_send()


COPIES = 120


def body(right_side, below_blocks, diag_cols, tile_home, block_rows, block_counts):
    vm = pltpu.VMEM
    anyspace = pl.BlockSpec(memory_space=pl.ANY)
    return pl.pallas_call(
        kernel,
        name="solve",
        out_shape=jax.ShapeDtypeStruct((2, 256, TILE), F32),
        in_specs=[pl.BlockSpec(memory_space=pltpu.SMEM), anyspace, anyspace, anyspace],
        out_specs=pl.BlockSpec(memory_space=pltpu.VMEM),
        scratch_shapes=[
            vm((4, 2, ROWS, TILE), F32),
            vm((4, 4, 256, TILE), F32),
            vm((4, 4, 256, TILE), F32),
            vm((2, 4, 4, TILE, 256), F32),
            vm((2, 4, 4, TILE, 256), F32),
            vm((4, 1024, 256), BF16),
            vm((4, 1024, 256), BF16),
            vm((4, 1024, 256), BF16),
            vm((4, 1024, 256), BF16),
            vm((ROWS, 1024), BF16),
            vm((ROWS, 1024), BF16),
            vm((3, 8, ROWS, TILE), F32),
            vm((3, 7, ROWS, TILE), F32),
            vm((3, ROWS, TILE), F32),
            vm((3, 8, ROWS, TILE), F32),
            vm((3, 4, ROWS, 256), F32),
            vm((3, 4, ROWS, 256), F32),
            vm((4, HALF, 256), F32),
            vm((4, ROWS, 256), F32),
            vm((4, 2, HALF, TILE), F32),
            vm((4, 2, HALF, TILE), F32),
            pltpu.SemaphoreType.DMA((COPIES,)),
            pltpu.SemaphoreType.DMA((COPIES,)),
            pltpu.SemaphoreType.DMA((8,)),
        ],
        compiler_params=pltpu.CompilerParams(
            collective_id=0, has_side_effects=True, vmem_limit_bytes=48 * 2**20
        ),
    )(masks(tile_home, block_rows, block_counts), right_side, below_blocks, diag_cols)


def solution(mesh):
    return jax.shard_map(
        body,
        mesh=mesh,
        in_specs=(
            P("blk", None, None),
            P("blk", None, None, "col"),
            P("blk", "col", None),
            P(),
            P(),
            P(),
        ),
        out_specs=P("blk", "col", None),
        check_vma=False,
    )
```

time: 681 us -> 159 us (0.23)
  waiting for transfers between devices: 590 us -> 0 us
  Pallas kernels: 0 us -> 152 us
  matrix products: 69.3 us -> 0 us
  between operations: 13.6 us -> 0.05 us
    psum x3 -> x0, waiting for transfers between devices: 453 us -> none  [body(): residual = lax.psum(partial_value, 'blk')]
    pallas_call x0 -> x1, Pallas kernels: none -> 152 us  [body(): pl.pallas_call(kernel, name='solve', out_shape=jax.ShapeDtypeStruct((2, 2...]
    reduce_scatter x3 -> x0, waiting for transfers between devices: 105 us -> none  [body(): solved = lax.psum_scatter(products, 'col', scatter_dimension=1, tiled=True)]
    dot_general x8 -> x0, matrix products: 69.3 us -> none  [the longest x3 43.8 us: body(): jnp.einsum('ju,jsb->sub', placing, right_side, precision=precise)]
    all_gather x2 -> x0, waiting for transfers between devices: 32 us -> none  [body(): gathered = gathered + lax.all_gather(solved, 'col', axis=1, tiled=True)]
  transfers between devices with their start and end apart: 8 -> 0, of which waited for: 8 -> 0; matrix products, arithmetic and copies ran while one was open for 4% -> 0% of each run, Pallas kernels for 0% -> 0%
where the time goes in v1:
time: 159 us
  Pallas kernels  152 us (96%)
  local copies, waits for them, and re-layouts  4.47 us (3%)
  other arithmetic  2.6 us (2%)
    pallas_call x1, Pallas kernels, body(): pl.pallas_call(kernel, name='solve', out_shape=jax.ShapeDtypeStruct((2, 2...  152 us
    unnamed x7, local copies, waits for them, and re-layouts  4.38 us

profile of v1, /device:TPU:1, one launch (start us, length us, event | category | flops | bytes accessed | tf_op | source)
XLA Modules:
  0.0 158.7 jit_solution(6319681105682661054)
XLA Ops:
  0.0 0.8 select_reduce_fusion
  0.9 0.7 iota_compare_fusion
  1.6 0.9 and_reduce_fusion
  2.5 0.1 broadcast_compare_fusion
  2.6 0.1 reshape.190.mask
  2.7 0.0 copy-start
  2.7 1.6 copy-done
  4.3 0.0 copy-start.1
  4.3 1.1 copy-done.1
  5.5 0.0 copy-start.2
  5.5 0.9 copy-done.2
  6.4 151.5 %solve.1 = f32[2,256,128]{2,1,0:T(8,128)S(1)} custom-call(f32[240]{0:T(256)S(1)} %reshape.190.mask, f32[2,2048,128]{2,1,0:T(8,128)S(1)} %copy-done, f32[2,3,128,256]{3,2,1,0:T(8,128)S(1)} %copy-done.1, f32[2,256,128]{2,1,0:T(8,128)S(1)} %copy-done.2), custom_call_target="tpu_custom_call" | custom-call | tf_op jit(solution)/shard_map/solve/pallas_call | solution.py:307
  157.9 0.7 copy.11
  (8 shorter events, 0.1 us)
Async XLA Ops:
  2.7 1.6 %copy-start = (f32[2,2048,128]{2,1,0:T(8,128)S(1)}, f32[2,2048,128]{2,1,0:T(8,128)}, u32[]{:S(2)}) copy-start(f32[2,2048,128]{2,1,0:T(8,128)} %rhs.1) | copy-start | bytes 6291460
  4.3 1.1 copy-start.1
  5.5 0.9 copy-start.2

commit v2 on v1

--- a/solution.py
+++ b/solution.py
@@ -1,5 +1,3 @@
-import functools
-
 import jax
 import jax.numpy as jnp
 from jax import lax
@@ -21,31 +19,14 @@
 BF16 = jnp.bfloat16
 
 
-def masks(tile_home, block_rows, block_counts):
-    z = lax.axis_index("blk") % NZ
-    core = lax.axis_index("col") % 2
-    order = jnp.arange(8, dtype=jnp.int32)
-    slots = ((order // 2) * NZ + z) * 2 + order % 2
-    matched = tile_home[None, :] == slots[:, None]
-    tile_of = jnp.max(jnp.where(matched, jnp.arange(TILES, dtype=jnp.int32)[None, :], -1), axis=1)
-    levels = jnp.arange(SUPERS, dtype=jnp.int32)
-    in_level = (tile_of[None, :] // TILES_SUP == levels[:, None]) & (tile_of >= 0)[None, :]
-    cols = 4 * (order // 2) + 2 * core + order % 2
-    placing = in_level[:, None, :] & (tile_of % TILES_SUP == cols[:, None])[None, :, :]
-    live = jnp.arange(MAX_BELOW, dtype=jnp.int32)[None, :] < block_counts[:, None]
-    hits = (block_rows[:, :, None] == tile_of[None, None, :]) & live[:, :, None]
-    present = jnp.any(hits, axis=1)
-    both = jnp.stack([in_level, present], axis=1)
-    return jnp.concatenate([placing, both], axis=1).astype(F32).reshape(SUPERS * 10 * 8)
-
-
 def split(v):
     hi = v.astype(BF16)
     return hi, (v - hi.astype(F32)).astype(BF16)
 
 
 def kernel(
-    mask, rhs, below, diag, out,
+    home_in, rows_in, counts_in, rhs, below, diag, out,
+    home, rows_ref, counts, mask,
     b8, df0, df1, lf0, lf1, dhi, dlo, lhi, llo, xhi, xlo,
     part, rbuf, chunk, res, spart, exch, exch0, sol, outs, outr,
     send, recv, local,
@@ -54,19 +35,24 @@
     y, z = blk // NZ, blk % NZ
     x, k = col // 2, col % 2
     count = [0, 0]
+    other = pl.ds(pl.multiple_of((1 - k) * HALF, HALF), HALF)
+    mine = pl.ds(pl.multiple_of(k * HALF, HALF), HALF)
 
     def at(dy=0, dz=0, dx=0, dk=0):
         return (((y + dy) % NY) * NZ + (z + dz) % NZ, ((x + dx) % NX) * 2 + (k + dk) % 2)
 
-    def push(src, dst, **where):
-        i = count[0]
-        count[0] += 1
+    def push(src, dst, slot=None, **where):
+        i = slot
+        if slot is None:
+            i = count[0]
+            count[0] += 1
         c = pltpu.make_async_remote_copy(
             src_ref=src, dst_ref=dst, send_sem=send.at[i], recv_sem=recv.at[i],
             device_id=at(**where), device_id_type=MESH,
         )
         c.start()
-        sent.append(c)
+        if slot is None:
+            sent.append(c)
         return c
 
     def keep(src, dst):
@@ -77,6 +63,7 @@
         return c
 
     sent = []
+    ints = [keep(home_in, home), keep(rows_in, rows_ref), keep(counts_in, counts)]
     own = [keep(diag.at[0], df0.at[y, x]), keep(diag.at[1], df1.at[x, y])]
     own_b = []
     for h in range(2):
@@ -107,26 +94,76 @@
                 )
             )
 
-    def first(src0, dst0, src1, dst1):
-        cs = []
+    def begin(a0, a1, own0, own1):
+        hop = {}
         for d in (1, 3, 2):
-            cs.append(push(src0, dst0, dx=d))
-            cs.append(push(src1, dst1, dy=d))
-        return cs
-
-    def second(src0, src1):
-        cs = []
-        for d in (1, 3, 2):
-            cs.append(push(src0, src0, dy=d))
-            cs.append(push(src1, src1, dx=d))
-        return cs
+            hop["x", d] = push(own0, a0.at[y, x], dx=d)
+            hop["y", d] = push(own1, a1.at[x, y], dy=d)
+        for d in (1, 3):
+            hop["yy", d, 0] = push(own0, a0.at[y, x], dy=d)
+            hop["xx", d, 0] = push(own1, a1.at[x, y], dx=d)
+        return a0, a1, hop
+
+    def forward(st):
+        a0, a1, hop = st
+        for e in (1, 3, 2):
+            hop.pop(("x", e)).wait_recv()
+            piece = a0.at[y, (x - e) % NX]
+            for d in (1, 3):
+                hop["yy", d, e] = push(piece, piece, dy=d)
+            hop.pop(("y", e)).wait_recv()
+            piece = a1.at[x, (y - e) % NY]
+            for d in (1, 3):
+                hop["xx", d, e] = push(piece, piece, dx=d)
+
+    def relay(st):
+        a0, a1, hop = st
+        for i in range(2):
+            for d, e in ((1, (0, 1)[i]), (3, (3, 2)[i])):
+                hop.pop(("yy", d, e)).wait_recv()
+                piece = a0.at[(y - d) % NY, (x - e) % NX]
+                hop["far y", d, e] = push(piece, piece, dy=d)
+                hop.pop(("xx", d, e)).wait_recv()
+                piece = a1.at[(x - d) % NX, (y - e) % NY]
+                hop["far x", d, e] = push(piece, piece, dx=d)
+
+    def finish(st):
+        for c in st[2].values():
+            c.wait_recv()
 
     def arrive(cs):
         for c in cs:
             c.wait_recv()
 
-    d_first = first(diag.at[0], df0.at[y, x], diag.at[1], df1.at[x, y])
-
+    sd = begin(df0, df1, diag.at[0], diag.at[1])
+
+    slots = [((i // 2) * NZ + z) * 2 + i % 2 for i in range(8)]
+
+    def find(r, tiles):
+        h = home[r]
+        return tuple(jnp.where(h == slots[i], r, tiles[i]) for i in range(8))
+
+    for c in ints:
+        c.wait()
+    tiles = lax.fori_loop(0, TILES, find, (jnp.int32(-1),) * 8, unroll=4)
+    for s in range(SUPERS):
+        used = counts[s]
+
+        def hit(e, found):
+            r = jnp.where(e < used, rows_ref[s, e], -2)
+            return tuple(jnp.where(r == tiles[i], 1.0, found[i]) for i in range(8))
+
+        found = lax.fori_loop(0, MAX_BELOW, hit, (jnp.float32(0.0),) * 8, unroll=4)
+        for i in range(8):
+            q = tiles[i] - s * TILES_SUP
+            inside = (q >= 0) & (q < TILES_SUP)
+            mask[(s * 10 + 8) * 8 + i] = jnp.where(inside, 1.0, 0.0)
+            mask[(s * 10 + 9) * 8 + i] = found[i]
+            for t in range(8):
+                col_tile = 4 * (t // 2) + 2 * k + t % 2
+                mask[(s * 10 + t) * 8 + i] = jnp.where(q == col_tile, 1.0, 0.0)
+
+    forward(sd)
     for c in own_b:
         c.wait()
     arrive(bcopies)
@@ -162,23 +199,17 @@
 
     place(2)
     rs = scatter(2)
-
-    for c in own:
-        c.wait()
-    arrive(d_first)
-    d_second = second(df0.at[y], df1.at[x])
-    l1_first = first(below.at[0, 1], lf0.at[1, y, x], below.at[1, 1], lf1.at[1, x, y])
+    relay(sd)
+    s1 = begin(lf0.at[1], lf1.at[1], below.at[0, 1], below.at[1, 1])
     place(1)
     place(0)
     arrive(rs)
     reduce(2)
     ag = gather(2)
-    arrive(d_second)
-    for c in own_l[0]:
+    forward(s1)
+    for c in own:
         c.wait()
-    arrive(l1_first)
-    l1_second = second(lf0.at[1, y], lf1.at[1, x])
-    l0_first = first(below.at[0, 0], lf0.at[0, y, x], below.at[1, 0], lf1.at[0, x, y])
+    finish(sd)
 
     def convert_d(i, carry):
         a, b = i // 4, i % 4
@@ -214,19 +245,32 @@
             xhi[:, t * TILE:(t + 1) * TILE] = hi
             xlo[:, t * TILE:(t + 1) * TILE] = lo
 
+        base = count[0]
+        count[0] += 4
+
         def step(n, carry):
             spart[s, n] = product(dhi, dlo, n)
+            trade(s, n, base).start()
             return carry
 
         lax.fori_loop(0, 4, step, 0)
+        return base
+
+    def trade(s, n, base):
+        src, dst = (spart.at[s, n], exch.at[s, n]) if s else (spart.at[0, n, other, :], exch0.at[n])
+        return pltpu.make_async_remote_copy(
+            src_ref=src, dst_ref=dst, send_sem=send.at[base + n], recv_sem=recv.at[base + n],
+            device_id=at(dk=1), device_id_type=MESH,
+        )
 
     def lanes(s, row, n):
         lane = lax.broadcasted_iota(jnp.int32, (1, 256), 1)
         base = (s * 10 + row) * 8 + 2 * n
         return jnp.where(lane < TILE, mask[base], mask[base + 1])
 
-    def absorb(s, target):
+    def absorb(s, target, ex):
         def step(n, carry):
+            trade(s, n, ex).wait()
             v = jnp.where(lanes(s, 8, n) > 0.5, spart[s, n] + exch[s, n], 0.0)
             if s < SUPERS - 1:
                 v = v + sol[n]
@@ -249,41 +293,37 @@
         lax.fori_loop(0, 4, step, 0)
 
     lax.fori_loop(0, 16, convert_d, 0)
+    relay(s1)
+    s0 = begin(lf0.at[0], lf1.at[0], below.at[0, 0], below.at[1, 0])
     arrive(ag)
-    diag_step(2)
-    ex = push(spart.at[2], exch.at[2], dk=1)
-    for c in own_l[1]:
-        c.wait()
-    arrive(l0_first)
-    arrive(l1_second)
-    l0_second = second(lf0.at[0, y], lf1.at[0, x])
+    ex = diag_step(2)
+    forward(s0)
+    for c in own_l:
+        for w in c:
+            w.wait()
+    finish(s1)
     convert_l(1)
-    ex.wait_recv()
-    absorb(2, 1)
+    absorb(2, 1, ex)
     below_step(1)
     rs = scatter(1)
+    relay(s0)
     arrive(rs)
     reduce(1)
     ag = gather(1)
-    arrive(l0_second)
+    finish(s0)
     convert_l(0)
     arrive(ag)
-    diag_step(1)
-    ex = push(spart.at[1], exch.at[1], dk=1)
-    ex.wait_recv()
-    absorb(1, 0)
+    ex = diag_step(1)
+    absorb(1, 0, ex)
     below_step(0)
     rs = scatter(0)
     arrive(rs)
     reduce(0)
     ag = gather(0)
     arrive(ag)
-    diag_step(0)
-    other = pl.ds(pl.multiple_of((1 - k) * HALF, HALF), HALF)
-    mine = pl.ds(pl.multiple_of(k * HALF, HALF), HALF)
-    ex = push(spart.at[0, :, other, :], exch0, dk=1)
-    ex.wait_recv()
+    ex = diag_step(0)
     for n in range(4):
+        trade(0, n, ex).wait()
         v = spart[0, n, mine, :] + exch0[n]
         v = sol[n, mine, :] + jnp.where(lanes(0, 8, n) > 0.5, v, 0.0)
         outs[n, 0] = v[:, :TILE]
@@ -298,19 +338,23 @@
         c.wait_send()
 
 
-COPIES = 120
+COPIES = 180
 
 
 def body(right_side, below_blocks, diag_cols, tile_home, block_rows, block_counts):
     vm = pltpu.VMEM
-    anyspace = pl.BlockSpec(memory_space=pl.ANY)
+    hbm = pl.BlockSpec(memory_space=pltpu.HBM)
     return pl.pallas_call(
         kernel,
         name="solve",
         out_shape=jax.ShapeDtypeStruct((2, 256, TILE), F32),
-        in_specs=[pl.BlockSpec(memory_space=pltpu.SMEM), anyspace, anyspace, anyspace],
+        in_specs=[hbm] * 6,
         out_specs=pl.BlockSpec(memory_space=pltpu.VMEM),
         scratch_shapes=[
+            pltpu.SMEM((TILES,), jnp.int32),
+            pltpu.SMEM((SUPERS, MAX_BELOW), jnp.int32),
+            pltpu.SMEM((SUPERS,), jnp.int32),
+            pltpu.SMEM((SUPERS * 10 * 8,), F32),
             vm((4, 2, ROWS, TILE), F32),
             vm((4, 4, 256, TILE), F32),
             vm((4, 4, 256, TILE), F32),
@@ -334,12 +378,12 @@
             vm((4, 2, HALF, TILE), F32),
             pltpu.SemaphoreType.DMA((COPIES,)),
             pltpu.SemaphoreType.DMA((COPIES,)),
-            pltpu.SemaphoreType.DMA((8,)),
+            pltpu.SemaphoreType.DMA((12,)),
         ],
         compiler_params=pltpu.CompilerParams(
-            collective_id=0, has_side_effects=True, vmem_limit_bytes=48 * 2**20
+            collective_id=0, has_side_effects=True, vmem_limit_bytes=60 * 2**20
         ),
-    )(masks(tile_home, block_rows, block_counts), right_side, below_blocks, diag_cols)
+    )(tile_home, block_rows, block_counts, right_side, below_blocks, diag_cols)
 
 
 def solution(mesh):

time: 159 us -> 140 us (0.88)
  Pallas kernels: 152 us -> 138 us
  local copies, waits for them, and re-layouts: 4.47 us -> 1.67 us
  other arithmetic: 2.6 us -> 0 us
    pallas_call x1, Pallas kernels: 152 us -> 138 us  [body(): pl.pallas_call(kernel, name='solve', out_shape=jax.ShapeDtypeStruct((2, 2...]
    unnamed x7 -> x1, local copies, waits for them, and re-layouts: 4.38 us -> 1.67 us
where the time goes in v2:
time: 140 us
  Pallas kernels  138 us (99%)
  local copies, waits for them, and re-layouts  1.67 us (1%)
    pallas_call x1, Pallas kernels, body(): pl.pallas_call(kernel, name='solve', out_shape=jax.ShapeDtypeStruct((2, 2...  138 us

profile of v2, /device:TPU:1, one launch (start us, length us, event | category | flops | bytes accessed | tf_op | source)
XLA Modules:
  0.0 139.9 jit_solution(6515143067096825547)
XLA Ops:
  0.0 138.2 %solve.1 = f32[2,256,128]{2,1,0:T(8,128)} custom-call(s32[48]{0:T(128)} %home_in.1, s32[3,32]{1,0:T(4,128)} %rows_in.1, s32[3]{0:T(128)} %counts_in.1, f32[2,2048,128]{2,1,0:T(8,128)} %rhs.1, f32[2,3,128,256]{3,2,1,0:T(8,128)} %below.1, f32[2,256,128]{2,1,0:T(8,128)} %diag.1), custom_call_target="tpu_custom_call" | custom-call | tf_op jit(solution)/shard_map/solve/pallas_call | solution.py:347
  138.2 1.7 %copy.8 = f32[2,256,128]{2,1,0:T(8,128)} copy(f32[2,256,128]{2,1,0:T(8,128)} %solve.1) | data formatting | bytes 524288

commit v3 on v2

--- a/solution.py
+++ b/solution.py
@@ -27,16 +27,14 @@
 def kernel(
     home_in, rows_in, counts_in, rhs, below, diag, out,
     home, rows_ref, counts, mask,
-    b8, df0, df1, lf0, lf1, dhi, dlo, lhi, llo, xhi, xlo,
-    part, rbuf, chunk, res, spart, exch, exch0, sol, outs, outr,
+    b8, df0, df1, lf0, lf1, dhi, dlo, lhi, llo, xd, xl,
+    part, rbuf, chunk, res, spart, exch, sol, outs, outr,
     send, recv, local,
 ):
     blk, col = lax.axis_index("blk"), lax.axis_index("col")
     y, z = blk // NZ, blk % NZ
     x, k = col // 2, col % 2
     count = [0, 0]
-    other = pl.ds(pl.multiple_of((1 - k) * HALF, HALF), HALF)
-    mine = pl.ds(pl.multiple_of(k * HALF, HALF), HALF)
 
     def at(dy=0, dz=0, dx=0, dk=0):
         return (((y + dy) % NY) * NZ + (z + dz) % NZ, ((x + dx) % NX) * 2 + (k + dk) % 2)
@@ -173,39 +171,34 @@
             acc = jnp.zeros((ROWS, TILE), F32)
             for i in range(8):
                 acc = acc + b8[i // 2, i % 2] * mask[(s * 10 + t) * 8 + i]
-            part[s, t] = acc
+            part[s, 0, t] = acc[:HALF]
+            part[s, 1, t] = acc[HALF:]
             return carry
 
         lax.fori_loop(0, 8, tile, 0)
 
-    def scatter(s):
+    def scatter(s, h):
         cs = []
         for d in (4, 3, 5, 2, 6, 1, 7):
-            cs.append(push(part.at[s, (z + d) % NZ], rbuf.at[s, d - 1], dz=d))
+            cs.append(push(part.at[s, h, (z + d) % NZ], rbuf.at[s, h, d - 1], dz=d))
         return cs
 
-    def reduce(s):
-        total = part[s, z]
+    def turn(s, h, cs):
+        arrive(cs)
+        total = part[s, h, z]
         for d in range(1, NZ):
-            total = total + rbuf[s, d - 1]
-        chunk[s] = total
-        res[s, z] = total
-
-    def gather(s):
-        cs = []
-        for d in (4, 3, 5, 2, 6, 1, 7):
-            cs.append(push(chunk.at[s], res.at[s, z], dz=d))
-        return cs
+            total = total + rbuf[s, h, d - 1]
+        chunk[s, h] = total
+        res[s, h, z] = total
+        return [push(chunk.at[s, h], res.at[s, h, z], dz=d) for d in (4, 3, 5, 2, 6, 1, 7)]
 
     place(2)
-    rs = scatter(2)
+    rs = [scatter(2, 0), scatter(2, 1)]
     relay(sd)
     s1 = begin(lf0.at[1], lf1.at[1], below.at[0, 1], below.at[1, 1])
     place(1)
     place(0)
-    arrive(rs)
-    reduce(2)
-    ag = gather(2)
+    ag = [turn(2, h, rs[h]) for h in range(2)]
     forward(s1)
     for c in own:
         c.wait()
@@ -232,34 +225,32 @@
 
         lax.fori_loop(0, 16, step, 0)
 
-    def product(whi, wlo, n):
-        a, b = xhi[...], xlo[...]
-        w = whi[n]
-        acc = jnp.dot(a, w, preferred_element_type=F32)
-        acc = acc + jnp.dot(b, w, preferred_element_type=F32)
-        return acc + jnp.dot(a, wlo[n], preferred_element_type=F32)
-
-    def diag_step(s):
+    def product(xs, whi, wlo, n):
+        both = jnp.dot(xs[...], whi[n], preferred_element_type=F32)
+        cross = jnp.dot(xs[:HALF], wlo[n], preferred_element_type=F32)
+        return both[:HALF] + (both[HALF:] + cross)
+
+    def diag_step(s, h, cs):
+        arrive(cs)
         for t in range(8):
-            hi, lo = split(res[s, t])
-            xhi[:, t * TILE:(t + 1) * TILE] = hi
-            xlo[:, t * TILE:(t + 1) * TILE] = lo
-
+            hi, lo = split(res[s, h, t])
+            xd[:HALF, t * TILE:(t + 1) * TILE] = hi
+            xd[HALF:, t * TILE:(t + 1) * TILE] = lo
         base = count[0]
         count[0] += 4
 
         def step(n, carry):
-            spart[s, n] = product(dhi, dlo, n)
-            trade(s, n, base).start()
+            spart[s, h, n] = product(xd, dhi, dlo, n)
+            trade(s, h, n, base).start()
             return carry
 
         lax.fori_loop(0, 4, step, 0)
         return base
 
-    def trade(s, n, base):
-        src, dst = (spart.at[s, n], exch.at[s, n]) if s else (spart.at[0, n, other, :], exch0.at[n])
+    def trade(s, h, n, base):
         return pltpu.make_async_remote_copy(
-            src_ref=src, dst_ref=dst, send_sem=send.at[base + n], recv_sem=recv.at[base + n],
+            src_ref=spart.at[s, h, n], dst_ref=exch.at[s, h, n],
+            send_sem=send.at[base + n], recv_sem=recv.at[base + n],
             device_id=at(dk=1), device_id_type=MESH,
         )
 
@@ -268,64 +259,58 @@
         base = (s * 10 + row) * 8 + 2 * n
         return jnp.where(lane < TILE, mask[base], mask[base + 1])
 
-    def absorb(s, target, ex):
+    def below_step(s, h, ex):
+        def weigh(n, carry):
+            trade(s + 1, h, n, ex).wait()
+            v = spart[s + 1, h, n] + exch[s + 1, h, n]
+            v = jnp.where(lanes(s + 1, 8, n) > 0.5, v, 0.0)
+            if s == 0:
+                v = v + sol[h, n]
+            sol[h, n] = v
+            hi, lo = split(v * lanes(s, 9, n))
+            where = pl.ds(pl.multiple_of(n * 256, 256), 256)
+            xl[:HALF, where] = hi
+            xl[HALF:, where] = lo
+            return carry
+
+        lax.fori_loop(0, 4, weigh, 0)
+
         def step(n, carry):
-            trade(s, n, ex).wait()
-            v = jnp.where(lanes(s, 8, n) > 0.5, spart[s, n] + exch[s, n], 0.0)
-            if s < SUPERS - 1:
-                v = v + sol[n]
-            sol[n] = v
-            hi, lo = split(v * lanes(target, 9, n))
-            where = pl.ds(pl.multiple_of(n * 256, 256), 256)
-            xhi[:, where] = hi
-            xlo[:, where] = lo
+            acc = product(xl, lhi, llo, n)
+            part[s, h, 2 * n] = part[s, h, 2 * n] - acc[:, :TILE]
+            part[s, h, 2 * n + 1] = part[s, h, 2 * n + 1] - acc[:, TILE:]
             return carry
 
         lax.fori_loop(0, 4, step, 0)
-
-    def below_step(s):
-        def step(n, carry):
-            acc = product(lhi, llo, n)
-            part[s, 2 * n] = part[s, 2 * n] - acc[:, :TILE]
-            part[s, 2 * n + 1] = part[s, 2 * n + 1] - acc[:, TILE:]
-            return carry
-
-        lax.fori_loop(0, 4, step, 0)
+        return scatter(s, h)
 
     lax.fori_loop(0, 16, convert_d, 0)
     relay(s1)
     s0 = begin(lf0.at[0], lf1.at[0], below.at[0, 0], below.at[1, 0])
-    arrive(ag)
-    ex = diag_step(2)
+    ex = [diag_step(2, h, ag[h]) for h in range(2)]
     forward(s0)
     for c in own_l:
         for w in c:
             w.wait()
     finish(s1)
     convert_l(1)
-    absorb(2, 1, ex)
-    below_step(1)
-    rs = scatter(1)
+    rs = [below_step(1, h, ex[h]) for h in range(2)]
     relay(s0)
-    arrive(rs)
-    reduce(1)
-    ag = gather(1)
+    ag = [turn(1, h, rs[h]) for h in range(2)]
     finish(s0)
     convert_l(0)
-    arrive(ag)
-    ex = diag_step(1)
-    absorb(1, 0, ex)
-    below_step(0)
-    rs = scatter(0)
-    arrive(rs)
-    reduce(0)
-    ag = gather(0)
-    arrive(ag)
-    ex = diag_step(0)
+    ex0 = diag_step(1, 0, ag[0])
+    rs0 = below_step(0, 0, ex0)
+    ex1 = diag_step(1, 1, ag[1])
+    rs1 = below_step(0, 1, ex1)
+    ag = [turn(0, 0, rs0), turn(0, 1, rs1)]
+    ex = [diag_step(0, h, ag[h]) for h in range(2)]
+    for h in range(2):
+        for n in range(4):
+            trade(0, h, n, ex[h]).wait()
     for n in range(4):
-        trade(0, n, ex).wait()
-        v = spart[0, n, mine, :] + exch0[n]
-        v = sol[n, mine, :] + jnp.where(lanes(0, 8, n) > 0.5, v, 0.0)
+        v = spart[0, k, n] + exch[0, k, n]
+        v = sol[k, n] + jnp.where(lanes(0, 8, n) > 0.5, v, 0.0)
         outs[n, 0] = v[:, :TILE]
         outs[n, 1] = v[:, TILE:]
     oc = [push(outs.at[(y + d) % NY], outr.at[y], dy=d) for d in (1, 3, 2)]
@@ -338,7 +323,7 @@
         c.wait_send()
 
 
-COPIES = 180
+COPIES = 240
 
 
 def body(right_side, below_blocks, diag_cols, tile_home, block_rows, block_counts):
@@ -366,14 +351,13 @@
             vm((4, 1024, 256), BF16),
             vm((ROWS, 1024), BF16),
             vm((ROWS, 1024), BF16),
-            vm((3, 8, ROWS, TILE), F32),
-            vm((3, 7, ROWS, TILE), F32),
-            vm((3, ROWS, TILE), F32),
-            vm((3, 8, ROWS, TILE), F32),
-            vm((3, 4, ROWS, 256), F32),
-            vm((3, 4, ROWS, 256), F32),
-            vm((4, HALF, 256), F32),
-            vm((4, ROWS, 256), F32),
+            vm((3, 2, 8, HALF, TILE), F32),
+            vm((3, 2, 7, HALF, TILE), F32),
+            vm((3, 2, HALF, TILE), F32),
+            vm((3, 2, 8, HALF, TILE), F32),
+            vm((3, 2, 4, HALF, 256), F32),
+            vm((3, 2, 4, HALF, 256), F32),
+            vm((2, 4, HALF, 256), F32),
             vm((4, 2, HALF, TILE), F32),
             vm((4, 2, HALF, TILE), F32),
             pltpu.SemaphoreType.DMA((COPIES,)),

time: 140 us -> 134 us (0.957)
  Pallas kernels: 138 us -> 132 us
    pallas_call x1, Pallas kernels: 138 us -> 132 us  [body(): pl.pallas_call(kernel, name='solve', out_shape=jax.ShapeDtypeStruct((2, 2...]
where the time goes in v3:
time: 134 us
  Pallas kernels  132 us (99%)
  local copies, waits for them, and re-layouts  1.67 us (1%)
    pallas_call x1, Pallas kernels, body(): pl.pallas_call(kernel, name='solve', out_shape=jax.ShapeDtypeStruct((2, 2...  132 us

profile of v3, /device:TPU:1, one launch (start us, length us, event | category | flops | bytes accessed | tf_op | source)
XLA Modules:
  0.0 133.8 jit_solution(339593738987946097)
XLA Ops:
  0.0 132.1 %solve.1 = f32[2,256,128]{2,1,0:T(8,128)} custom-call(s32[48]{0:T(128)} %home_in.1, s32[3,32]{1,0:T(4,128)} %rows_in.1, s32[3]{0:T(128)} %counts_in.1, f32[2,2048,128]{2,1,0:T(8,128)} %rhs.1, f32[2,3,128,256]{3,2,1,0:T(8,128)} %below.1, f32[2,256,128]{2,1,0:T(8,128)} %diag.1), custom_call_target="tpu_custom_call" | custom-call | tf_op jit(solution)/shard_map/solve/pallas_call | solution.py:332
  132.1 1.7 %copy.8 = f32[2,256,128]{2,1,0:T(8,128)} copy(f32[2,256,128]{2,1,0:T(8,128)} %solve.1) | data formatting | bytes 524288

commit v4 on v3

--- a/solution.py
+++ b/solution.py
@@ -286,20 +286,20 @@
 
     lax.fori_loop(0, 16, convert_d, 0)
     relay(s1)
+    ex = [diag_step(2, h, ag[h]) for h in range(2)]
     s0 = begin(lf0.at[0], lf1.at[0], below.at[0, 0], below.at[1, 0])
-    ex = [diag_step(2, h, ag[h]) for h in range(2)]
-    forward(s0)
     for c in own_l:
         for w in c:
             w.wait()
     finish(s1)
     convert_l(1)
     rs = [below_step(1, h, ex[h]) for h in range(2)]
+    forward(s0)
+    ag = [turn(1, h, rs[h]) for h in range(2)]
     relay(s0)
-    ag = [turn(1, h, rs[h]) for h in range(2)]
+    ex0 = diag_step(1, 0, ag[0])
     finish(s0)
     convert_l(0)
-    ex0 = diag_step(1, 0, ag[0])
     rs0 = below_step(0, 0, ex0)
     ex1 = diag_step(1, 1, ag[1])
     rs1 = below_step(0, 1, ex1)

time: 134 us -> 129 us (0.963)
  Pallas kernels: 132 us -> 127 us
    pallas_call x1, Pallas kernels: 132 us -> 127 us  [body(): pl.pallas_call(kernel, name='solve', out_shape=jax.ShapeDtypeStruct((2, 2...]
where the time goes in v4:
time: 129 us
  Pallas kernels  127 us (98%)
  local copies, waits for them, and re-layouts  1.67 us (1%)
    pallas_call x1, Pallas kernels, body(): pl.pallas_call(kernel, name='solve', out_shape=jax.ShapeDtypeStruct((2, 2...  127 us

profile of v4, /device:TPU:1, one launch (start us, length us, event | category | flops | bytes accessed | tf_op | source)
XLA Modules:
  0.0 128.7 jit_solution(15198803291497718309)
XLA Ops:
  0.0 127.0 %solve.1 = f32[2,256,128]{2,1,0:T(8,128)} custom-call(s32[48]{0:T(128)} %home_in.1, s32[3,32]{1,0:T(4,128)} %rows_in.1, s32[3]{0:T(128)} %counts_in.1, f32[2,2048,128]{2,1,0:T(8,128)} %rhs.1, f32[2,3,128,256]{3,2,1,0:T(8,128)} %below.1, f32[2,256,128]{2,1,0:T(8,128)} %diag.1), custom_call_target="tpu_custom_call" | custom-call | tf_op jit(solution)/shard_map/solve/pallas_call | solution.py:332
  127.0 1.7 %copy.8 = f32[2,256,128]{2,1,0:T(8,128)} copy(f32[2,256,128]{2,1,0:T(8,128)} %solve.1) | data formatting | bytes 524288

commit v5 on v4

--- a/solution.py
+++ b/solution.py
@@ -74,23 +74,17 @@
         )
 
     peers = [dict(dy=d) for d in range(1, NY)] + [dict(dx=d) for d in range(1, NX)]
-    peers += [dict(dz=d) for d in range(1, NZ)] + [dict(dk=1)]
+    peers += [dict(dz=d) for d in range(1, NZ)] + [dict(dk=1)] + [dict(dy=d, dk=1) for d in range(1, NY)]
     barrier = pltpu.get_barrier_semaphore()
     for p in peers:
         pl.semaphore_signal(barrier, inc=1, device_id=at(**p), device_id_type=MESH)
     pl.semaphore_wait(barrier, len(peers))
 
+    half = pl.ds(pl.multiple_of(k * HALF, HALF), HALF)
     bcopies = []
     for d in (1, 3, 2):
-        for h in range(2):
-            start = pl.multiple_of((2 * x + h) * 256 + ((y + d) % NY) * HALF, HALF)
-            bcopies.append(
-                push(
-                    rhs.at[:, pl.ds(start, HALF), :],
-                    b8.at[y, :, pl.ds(h * HALF, HALF), :],
-                    dy=d,
-                )
-            )
+        start = pl.multiple_of((2 * x + k) * 256 + ((y + d) % NY) * HALF, HALF)
+        bcopies.append(push(rhs.at[:, pl.ds(start, HALF), :], b8.at[y, :, half, :], dy=d))
 
     def begin(a0, a1, own0, own1):
         hop = {}
@@ -164,7 +158,12 @@
     forward(sd)
     for c in own_b:
         c.wait()
-    arrive(bcopies)
+    swaps = []
+    for d, c in zip((1, 3, 2), bcopies):
+        c.wait_recv()
+        piece = b8.at[(y - d) % NY, :, half, :]
+        swaps.append(push(piece, piece, dk=1))
+    arrive(swaps)
 
     def place(s):
         def tile(t, carry):
@@ -230,12 +229,15 @@
         cross = jnp.dot(xs[:HALF], wlo[n], preferred_element_type=F32)
         return both[:HALF] + (both[HALF:] + cross)
 
-    def diag_step(s, h, cs):
+    def fill(s, h, cs):
         arrive(cs)
         for t in range(8):
             hi, lo = split(res[s, h, t])
             xd[:HALF, t * TILE:(t + 1) * TILE] = hi
             xd[HALF:, t * TILE:(t + 1) * TILE] = lo
+
+    def diag_step(s, h, cs):
+        fill(s, h, cs)
         base = count[0]
         count[0] += 4
 
@@ -304,21 +306,58 @@
     ex1 = diag_step(1, 1, ag[1])
     rs1 = below_step(0, 1, ex1)
     ag = [turn(0, 0, rs0), turn(0, 1, rs1)]
-    ex = [diag_step(0, h, ag[h]) for h in range(2)]
+    base = count[0]
+    count[0] += 16
+
+    def last(h, d):
+        rel = (h + k) % 2
+        return pltpu.make_async_remote_copy(
+            src_ref=outs.at[h, (y + d) % NY], dst_ref=outr.at[rel, y],
+            send_sem=send.at[base + 4 * h + d], recv_sem=recv.at[base + 8 + 4 * rel + d],
+            device_id=(((y + d) % NY) * NZ + z, x * 2 + h), device_id_type=MESH,
+        )
+
+    def landed(rel, d):
+        return pltpu.make_async_remote_copy(
+            src_ref=outs.at[0, y], dst_ref=outr.at[rel, (y - d) % NY],
+            send_sem=send.at[base + 8 + 4 * rel + d], recv_sem=recv.at[base + 8 + 4 * rel + d],
+            device_id=at(dy=d, dk=rel), device_id_type=MESH,
+        )
+
     for h in range(2):
-        for n in range(4):
-            trade(0, h, n, ex[h]).wait()
+        fill(0, h, ag[h])
+
+        def closing(n, carry):
+            v = jnp.where(lanes(0, 8, n) > 0.5, product(xd, dhi, dlo, n), 0.0)
+            mine = jnp.full((1, 256), jnp.where(k == h, 1.0, 0.0), F32) > 0.5
+            outs[h, n] = v + jnp.where(mine, sol[h, n], 0.0)
+            return carry
+
+        lax.fori_loop(0, 4, closing, 0)
+        for d in (1, 3, 2):
+            last(h, d).start()
+
+        @pl.when(k != h)
+        def _():
+            last(h, 0).start()
+
+    outr[0, y] = outs[k, y]
+    for rel in range(2):
+        for d in (1, 3, 2, 0):
+            if rel or d:
+                landed(rel, d).wait_recv()
     for n in range(4):
-        v = spart[0, k, n] + exch[0, k, n]
-        v = sol[k, n] + jnp.where(lanes(0, 8, n) > 0.5, v, 0.0)
-        outs[n, 0] = v[:, :TILE]
-        outs[n, 1] = v[:, TILE:]
-    oc = [push(outs.at[(y + d) % NY], outr.at[y], dy=d) for d in (1, 3, 2)]
-    outr[y] = outs[y]
-    arrive(oc)
-    for n in range(4):
+        v = outr[0, n] + outr[1, n]
         for j in range(2):
-            out[j, n * HALF:(n + 1) * HALF, :] = outr[n, j]
+            out[j, n * HALF:(n + 1) * HALF, :] = v[:, j * TILE:(j + 1) * TILE]
+    for h in range(2):
+        for d in (1, 3, 2):
+            last(h, d).wait_send()
+
+        @pl.when(k != h)
+        def _():
+            last(h, 0).wait_send()
+
     for c in sent:
         c.wait_send()
 
@@ -358,8 +397,8 @@
             vm((3, 2, 4, HALF, 256), F32),
             vm((3, 2, 4, HALF, 256), F32),
             vm((2, 4, HALF, 256), F32),
-            vm((4, 2, HALF, TILE), F32),
-            vm((4, 2, HALF, TILE), F32),
+            vm((2, 4, HALF, 256), F32),
+            vm((2, 4, HALF, 256), F32),
             pltpu.SemaphoreType.DMA((COPIES,)),
             pltpu.SemaphoreType.DMA((COPIES,)),
             pltpu.SemaphoreType.DMA((12,)),

time: 129 us -> 124 us (0.961)
  Pallas kernels: 127 us -> 122 us
    pallas_call x1, Pallas kernels: 127 us -> 122 us  [body(): pl.pallas_call(kernel, name='solve', out_shape=jax.ShapeDtypeStruct((2, 2...]
where the time goes in v5:
time: 124 us
  Pallas kernels  122 us (98%)
  local copies, waits for them, and re-layouts  1.67 us (1%)
    pallas_call x1, Pallas kernels, body(): pl.pallas_call(kernel, name='solve', out_shape=jax.ShapeDtypeStruct((2, 2...  122 us

profile of v5, /device:TPU:1, one launch (start us, length us, event | category | flops | bytes accessed | tf_op | source)
XLA Modules:
  0.0 124.0 jit_solution(16333900103887622996)
XLA Ops:
  0.0 122.4 %solve.1 = f32[2,256,128]{2,1,0:T(8,128)} custom-call(s32[48]{0:T(128)} %home_in.1, s32[3,32]{1,0:T(4,128)} %rows_in.1, s32[3]{0:T(128)} %counts_in.1, f32[2,2048,128]{2,1,0:T(8,128)} %rhs.1, f32[2,3,128,256]{3,2,1,0:T(8,128)} %below.1, f32[2,256,128]{2,1,0:T(8,128)} %diag.1), custom_call_target="tpu_custom_call" | custom-call | tf_op jit(solution)/shard_map/solve/pallas_call | solution.py:371
  122.4 1.7 %copy.8 = f32[2,256,128]{2,1,0:T(8,128)} copy(f32[2,256,128]{2,1,0:T(8,128)} %solve.1) | data formatting | bytes 524288

commit v6 on v5

--- a/solution.py
+++ b/solution.py
@@ -156,6 +156,7 @@
                 mask[(s * 10 + t) * 8 + i] = jnp.where(q == col_tile, 1.0, 0.0)
 
     forward(sd)
+    s1 = begin(lf0.at[1], lf1.at[1], below.at[0, 1], below.at[1, 1])
     for c in own_b:
         c.wait()
     swaps = []
@@ -194,11 +195,10 @@
     place(2)
     rs = [scatter(2, 0), scatter(2, 1)]
     relay(sd)
-    s1 = begin(lf0.at[1], lf1.at[1], below.at[0, 1], below.at[1, 1])
+    forward(s1)
     place(1)
     place(0)
     ag = [turn(2, h, rs[h]) for h in range(2)]
-    forward(s1)
     for c in own:
         c.wait()
     finish(sd)
@@ -277,14 +277,33 @@
 
         lax.fori_loop(0, 4, weigh, 0)
 
-        def step(n, carry):
+        base = count[0]
+        count[0] += NZ
+
+        def tile(t, d):
+            return pltpu.make_async_remote_copy(
+                src_ref=part.at[s, h, t], dst_ref=rbuf.at[s, h, d - 1],
+                send_sem=send.at[base + d], recv_sem=recv.at[base + d],
+                device_id=(y * NZ + t, col), device_id_type=MESH,
+            )
+
+        def step(i, carry):
+            n = (z // 2 + 2 + i) % 4
             acc = product(xl, lhi, llo, n)
-            part[s, h, 2 * n] = part[s, h, 2 * n] - acc[:, :TILE]
-            part[s, h, 2 * n + 1] = part[s, h, 2 * n + 1] - acc[:, TILE:]
+            for j in range(2):
+                t = 2 * n + j
+                part[s, h, t] = part[s, h, t] - acc[:, j * TILE:(j + 1) * TILE]
+
+                @pl.when(t != z)
+                def _():
+                    tile(t, (t - z + NZ) % NZ).start()
+
             return carry
 
         lax.fori_loop(0, 4, step, 0)
-        return scatter(s, h)
+        cs = [tile((z + d) % NZ, d) for d in range(1, NZ)]
+        sent.extend(cs)
+        return cs
 
     lax.fori_loop(0, 16, convert_d, 0)
     relay(s1)

time: 124 us -> 123 us (level)
    pallas_call x1, Pallas kernels: 122 us -> 121 us  [body(): pl.pallas_call(kernel, name='solve', out_shape=jax.ShapeDtypeStruct((2, 2...]
where the time goes in v6:
time: 123 us; the launch traced here: 122 us
  Pallas kernels  121 us (98%)
  local copies, waits for them, and re-layouts  1.67 us (1%)
    pallas_call x1, Pallas kernels, body(): pl.pallas_call(kernel, name='solve', out_shape=jax.ShapeDtypeStruct((2, 2...  121 us

profile of v6, /device:TPU:1, one launch (start us, length us, event | category | flops | bytes accessed | tf_op | source)
XLA Modules:
  0.0 122.5 jit_solution(8537257397492063025)
XLA Ops:
  0.0 120.8 %solve.1 = f32[2,256,128]{2,1,0:T(8,128)} custom-call(s32[48]{0:T(128)} %home_in.1, s32[3,32]{1,0:T(4,128)} %rows_in.1, s32[3]{0:T(128)} %counts_in.1, f32[2,2048,128]{2,1,0:T(8,128)} %rhs.1, f32[2,3,128,256]{3,2,1,0:T(8,128)} %below.1, f32[2,256,128]{2,1,0:T(8,128)} %diag.1), custom_call_target="tpu_custom_call" | custom-call | tf_op jit(solution)/shard_map/solve/pallas_call | solution.py:390
  120.8 1.7 %copy.8 = f32[2,256,128]{2,1,0:T(8,128)} copy(f32[2,256,128]{2,1,0:T(8,128)} %solve.1) | data formatting | bytes 524288

commit v7 on v6

--- a/solution.py
+++ b/solution.py
@@ -119,6 +119,11 @@
                 piece = a1.at[(x - d) % NX, (y - e) % NY]
                 hop["far x", d, e] = push(piece, piece, dx=d)
 
+    def near(st):
+        hop = st[2]
+        for key in [key for key in hop if key[0] in ("yy", "xx")]:
+            hop.pop(key).wait_recv()
+
     def finish(st):
         for c in st[2].values():
             c.wait_recv()
@@ -212,17 +217,17 @@
             dlo[a, rows, j * TILE:(j + 1) * TILE] = lo
         return carry
 
-    def convert_l(s):
+    def convert_l(s, first, steps):
         def step(i, carry):
-            a, b = i // 4, i % 4
-            for j, v in ((0, lf0[s, a, b]), (1, lf1[s, b, a])):
-                hi, lo = split(v)
+            far, same = first + i // 4, i % 4
+            for j, a, b in ((0, (y + far) % NY, same), (1, same, (x + far) % NX)):
+                hi, lo = split(lf1[s, b, a] if j else lf0[s, a, b])
                 rows = pl.ds(pl.multiple_of(a * 256 + j * TILE, TILE), TILE)
                 lhi[b, rows, :] = hi
                 llo[b, rows, :] = lo
             return carry
 
-        lax.fori_loop(0, 16, step, 0)
+        lax.fori_loop(0, steps, step, 0)
 
     def product(xs, whi, wlo, n):
         both = jnp.dot(xs[...], whi[n], preferred_element_type=F32)
@@ -312,15 +317,19 @@
     for c in own_l:
         for w in c:
             w.wait()
+    near(s1)
+    convert_l(1, 3, 12)
     finish(s1)
-    convert_l(1)
+    convert_l(1, 2, 4)
     rs = [below_step(1, h, ex[h]) for h in range(2)]
     forward(s0)
     ag = [turn(1, h, rs[h]) for h in range(2)]
     relay(s0)
+    near(s0)
+    convert_l(0, 3, 12)
     ex0 = diag_step(1, 0, ag[0])
     finish(s0)
-    convert_l(0)
+    convert_l(0, 2, 4)
     rs0 = below_step(0, 0, ex0)
     ex1 = diag_step(1, 1, ag[1])
     rs1 = below_step(0, 1, ex1)

time: 123 us -> 122 us (level)
  no operation moved by 1% of the time
where the time goes in v7:
time: 122 us
  Pallas kernels  120 us (98%)
  local copies, waits for them, and re-layouts  1.67 us (1%)
    pallas_call x1, Pallas kernels, body(): pl.pallas_call(kernel, name='solve', out_shape=jax.ShapeDtypeStruct((2, 2...  120 us

profile of v7, /device:TPU:1, one launch (start us, length us, event | category | flops | bytes accessed | tf_op | source)
XLA Modules:
  0.0 122.0 jit_solution(10372400592163080720)
XLA Ops:
  0.0 120.3 %solve.1 = f32[2,256,128]{2,1,0:T(8,128)} custom-call(s32[48]{0:T(128)} %home_in.1, s32[3,32]{1,0:T(4,128)} %rows_in.1, s32[3]{0:T(128)} %counts_in.1, f32[2,2048,128]{2,1,0:T(8,128)} %rhs.1, f32[2,3,128,256]{3,2,1,0:T(8,128)} %below.1, f32[2,256,128]{2,1,0:T(8,128)} %diag.1), custom_call_target="tpu_custom_call" | custom-call | tf_op jit(solution)/shard_map/solve/pallas_call | solution.py:399
  120.3 1.7 %copy.8 = f32[2,256,128]{2,1,0:T(8,128)} copy(f32[2,256,128]{2,1,0:T(8,128)} %solve.1) | data formatting | bytes 524288
